TPU v7x, 768 devices: a whole 4x8x12 slice. The times are simulated.
768 devices in a mesh: dp: 96 (over y, z), mp: 8 (over x, core).
Axes of the slice: x: 4, y: 8, z: 12, core: 2. Of those that a mesh axis runs over, the one named last changes fastest.
Arguments:
- hidden_acts: bfloat16 [30720, 15360], P('dp', 'mp'), may hold values from -20 to 20
- out_grad: bfloat16 [30720, 6144], P('dp'), may hold values from -6 to 6
- basis: bfloat16 [6144, 512], replicated, may hold values from -0.078125 to 0.078125
- code_first: int32 [15360, 512], P(('mp', 'dp')), may hold values from -127 to 127
- scale_first: float32 [15360, 2], P(('mp', 'dp')), may hold values from 0.05 to 0.3
- code_second: int32 [15360, 512], P(('mp', 'dp')), may hold values from 16 to 255
- scale_second: float32 [15360, 2], P(('mp', 'dp')), may hold values from 0.0005 to 0.004
Outputs:
- weight_update: bfloat16 [15360, 6144], P('mp', 'dp')
- first_new: float32 [15360, 512], P(('mp', 'dp'))
- second_new: float32 [15360, 512], P(('mp', 'dp'))
All inputs are finite; a program needn't handle non-finite values.
Results may differ from a plain program's by a relative error of at most 0.011.
Values may be sent and summed in bfloat16 or wider, within the bound.
A program may use at most 64 MiB of HBM per device.

v0:
```python
import math

import jax
import jax.numpy as jnp
from jax import lax
from jax.sharding import PartitionSpec as P


def dequant(codes, scales):
    row_count = codes.shape[0]
    block_len = codes.shape[1] // scales.shape[1]
    shaped = codes.astype(jnp.float32).reshape(row_count, scales.shape[1], block_len)
    return (shaped, scales[:, :, None])


def per_device(hidden_acts, out_grad, basis, code_first, scale_first, code_second, scale_second):
    tok_rows = out_grad.shape[0]
    factor = jnp.dot(out_grad, basis, preferred_element_type=jnp.float32).astype(jnp.bfloat16)
    dims = (((0,), (0,)), ((), ()))
    projected = lax.dot_general(hidden_acts, factor, dims, preferred_element_type=jnp.float32)
    grad_shard = lax.psum_scatter(projected, "dp", scatter_dimension=0, tiled=True)
    low_grad = grad_shard / math.sqrt(tok_rows * lax.axis_size("dp"))
    shaped_first, block_first = dequant(code_first, scale_first)
    first_old = (shaped_first / 127.0 * block_first).reshape(code_first.shape)
    shaped_second, block_second = dequant(code_second, scale_second)
    second_old = ((shaped_second / 255.0) ** 2 * block_second).reshape(code_second.shape)
    first_new = 0.9 * first_old + 0.1 * low_grad
    second_new = 0.999 * second_old + 0.001 * low_grad * low_grad
    normalized = (first_new / 0.19 / (jnp.sqrt(second_new / 0.001999) + 1e-08)).astype(jnp.bfloat16)
    gathered = lax.all_gather(normalized, "dp", axis=0, tiled=True)
    col_width = basis.shape[0] // lax.axis_size("dp")
    own_basis = lax.dynamic_slice_in_dim(basis, lax.axis_index("dp") * col_width, col_width, 0)
    weight_update = lax.dot_general(
        gathered, own_basis, (((1,), (1,)), ((), ())), preferred_element_type=jnp.float32
    ).astype(jnp.bfloat16)
    return (weight_update, first_new, second_new)


def solution(mesh):
    placed = (
        P("dp", "mp"),
        P("dp", None),
        P(),
        P(("mp", "dp"), None),
        P(("mp", "dp"), None),
        P(("mp", "dp"), None),
        P(("mp", "dp"), None),
    )
    return jax.shard_map(
        per_device,
        mesh=mesh,
        in_specs=placed,
        out_specs=(P("mp", "dp"), P(("mp", "dp"), None), P(("mp", "dp"), None)),
        check_vma=False,
    )
```

profile of v0, /device:TPU:6, one launch (start us, length us, event | category | flops | bytes accessed | tf_op | source)
XLA Modules:
  0.0 410.0 jit_solution(10396959181943658830)
XLA Ops:
  7.2 0.0 copy-start
  7.2 0.0 all-reduce.3.cloned.1.call-start
  7.2 1.2 copy-done
  8.5 9.3 %convolution_bitcast_fusion = f32[1920,512]{0,1:T(8,128)} fusion(bf16[320,1920]{1,0:T(8,128)(2,1)S(1)} %copy-done, bf16[320,6144]{1,0:T(8,128)(2,1)} %param.8, bf16[6144,512]{1,0:T(8,128)(2,1)} %param.9), kind=kOutput, calls=%fused_computation | convolution fusion | flops 2642575360 | bytes 15384576 | tf_op jit(solution)/shard_map/dot_general | solution.py:20
  17.7 0.0 copy-start.3
  17.8 0.0 all-reduce.3.cloned.1.call-update
  17.8 0.0 all-gather.3.cloned.1.call-start
  17.8 0.6 copy-done.3
  18.4 0.1 copy.24
  18.5 0.1 mul.58
  18.7 0.0 copy-done.4
  18.7 0.1 copy.26
  18.8 0.1 mul.65
  18.9 1.3 dynamic-slice
  20.8 253.2 %all-reduce.3.cloned.1.call-done = f32[1920,512]{0,1:T(8,128)} async-done(((f32[1920,512]{0,1:T(8,128)}), f32[1920,512]{0,1:T(8,128)}) %all-reduce.3.cloned.1.call-update) | async-done | bytes 3932176
  274.1 1.2 constant_dynamic-slice_fusion
  275.2 0.1 copy.25
  275.3 0.0 copy-done.1
  275.3 0.0 copy-done.2
  275.4 0.7 fusion.1
  276.0 0.0 all-gather.3.cloned.1.call-update
  276.1 122.3 %all-gather.3.cloned.1.call-done = bf16[96,20,512]{2,1,0:T(8,128)(2,1)} async-done(((bf16[1,20,512]{2,1,0:T(8,128)(2,1)}), bf16[96,20,512]{2,1,0:T(8,128)(2,1)}) %all-gather.3.cloned.1.call-update) | async-done | bytes 1966096 | tf_op jit(solution)/shard_map/all_gather | solution.py:30
  398.3 2.6 reshape.15
  400.9 2.3 convolution_convert_fusion
  (8 shorter events, 0.1 us)
Async XLA Ops:
  7.2 1.3 copy-start
  7.2 266.9 %all-reduce.3.cloned.1.call-start = ((), (), s32[]{:S(2)}) async-start(), calls=%async_computation.1 | async-start | bytes 7864320
  17.7 0.7 copy-start.3
  17.7 0.9 copy-start.4
  17.8 257.6 %copy-start.1 = (s32[20,512]{1,0:T(8,128)S(1)}, s32[20,512]{1,0:T(8,128)}, u32[]{:S(2)}) copy-start(s32[20,512]{1,0:T(8,128)} %param.10) | copy-start | bytes 122884
  17.8 257.6 %copy-start.2 = (s32[20,512]{1,0:T(8,128)S(1)}, s32[20,512]{1,0:T(8,128)}, u32[]{:S(2)}) copy-start(s32[20,512]{1,0:T(8,128)} %param.12) | copy-start | bytes 122884
  17.8 380.6 %all-gather.3.cloned.1.call-start = ((), (), s32[]{:S(2)}) async-start(), calls=%async_computation | async-start | bytes 2383872 | tf_op jit(solution)/shard_map/all_gather | solution.py:30
Sparse Core Ops, SparseCore 0:
  17.9 256.1 all-reduce.2
  278.4 119.9 all-gather.2
where the time goes:
time: 410 us
  waiting for transfers between devices  376 us (92%)
  between operations  14.8 us (4%)
  matrix products  11.6 us (3%)
  local copies, waits for them, and re-layouts  7.36 us (2%)
    unnamed x3, waiting for transfers between devices  253 us
    all_gather x1, waiting for transfers between devices, per_device(): gathered = lax.all_gather(normalized, 'dp', axis=0, tiled=True)  122 us
    dot_general x1, matrix products, per_device(): lax.dot_general(hidden_acts, factor, dims, preferred_element_type=jnp.flo...  9.29 us
  transfers between devices with their start and end apart: 2, of which 2 were waited for; matrix products, arithmetic and copies ran while one was open for 0% of the time, Pallas kernels for 0%

commit v1 on v0

v1 whole, which is shorter than its diff:
```python
import functools
import math

import jax
import jax.numpy as jnp
from jax import lax
from jax.experimental import pallas as pl
from jax.experimental.pallas import tpu as pltpu
from jax.sharding import PartitionSpec as P

NY, NZ = 8, 12
BLK = 20
RANK = 512
LANES = 128
G = RANK // LANES
PACK = G * BLK
KC = 8
F32, BF16 = jnp.float32, jnp.bfloat16
MESH = pl.DeviceIdType.MESH


def far_first(n):
    order = []
    for k in range(n // 2, 0, -1):
        order.append(k)
        if k != n - k:
            order.append(n - k)
    return order


def kernel(hid_hbm, og_hbm, bas_hbm, c1_hbm, s1_hbm, c2_hbm, s2_hbm,
           w_ref, m_ref, v_ref,
           hid, og, bas, c1, s1, c2, s2,
           htf, hperm, ht, acc, fac, proj, m_old, v_old,
           ring_y, ring_z, fresh_y, fresh_z, sumf, msg, land,
           stack, norm, gat, rowsf, bsel, wsend, wland,
           load_sem, send1, recv1, send2, recv2, send3, recv3, send4, recv4, *, tokens):
    dp, mp = lax.axis_index("dp"), lax.axis_index("mp")
    y, z = dp // NZ, dp % NZ
    core = mp % 2
    tok, ff = hid.shape
    kw = og.shape[2]

    def dev(yy, zz):
        return (yy * NZ + zz, mp)

    def at_y(k):
        return dev((y + k) % NY, z)

    def at_z(k):
        return dev(y, (z + k) % NZ)

    loads = [pltpu.make_async_copy(hid_hbm, hid, load_sem.at[0])]
    for k in range(KC):
        loads.append(pltpu.make_async_copy(og_hbm.at[:, pl.ds(k * kw, kw)], og.at[k], load_sem.at[1 + k]))
        loads.append(pltpu.make_async_copy(bas_hbm.at[pl.ds(k * kw, kw)], bas.at[pl.ds(k * kw, kw)], load_sem.at[1 + KC + k]))
    small = [(c1_hbm, c1), (s1_hbm, s1), (c2_hbm, c2), (s2_hbm, s2)]
    small = [pltpu.make_async_copy(a, b, load_sem.at[1 + 2 * KC + i]) for i, (a, b) in enumerate(small)]
    for c in loads + small:
        c.start()

    barrier = pltpu.get_barrier_semaphore()
    for k in range(1, NY):
        pl.semaphore_signal(barrier, inc=1, device_id=at_y(k), device_id_type=MESH)
    for k in range(1, NZ):
        pl.semaphore_signal(barrier, inc=1, device_id=at_z(k), device_id_type=MESH)

    loads[0].wait()
    for c in range(ff // LANES):
        htf[c * LANES:(c + 1) * LANES, :] = hid[:, c * LANES:(c + 1) * LANES].astype(F32).T

    @pl.when(core == 0)
    def _():
        ht[...] = htf[...].astype(BF16)

    @pl.when(core == 1)
    def _():
        for zz in range(NZ):
            for yy in range(NY):
                at = yy * NZ * BLK + zz * BLK
                hperm[yy * BLK:(yy + 1) * BLK, :] = htf[at:at + BLK, :]
            ht[zz * NY * BLK:(zz + 1) * NY * BLK, :] = hperm[...].astype(BF16)

    for k in range(KC):
        loads[1 + 2 * k].wait()
        loads[2 + 2 * k].wait()
        part = jnp.dot(og[k], bas[k * kw:(k + 1) * kw, :], preferred_element_type=F32)
        if k == 0:
            acc[...] = part
        elif k < KC - 1:
            acc[...] += part
        else:
            fac[...] = (acc[...] + part).astype(BF16)

    pl.semaphore_wait(barrier, NY - 1 + NZ - 1)

    def moments():
        for c in small:
            c.wait()
        eye = lax.broadcasted_iota(jnp.int32, (BLK, BLK), 0) == lax.broadcasted_iota(jnp.int32, (BLK, BLK), 1)
        half = RANK // 2
        for b in range(2):
            cols = slice(b * half, (b + 1) * half)
            sc1 = jnp.sum(jnp.where(eye, s1[b:b + 1, :], 0.0), axis=1, keepdims=True)
            sc2 = jnp.sum(jnp.where(eye, s2[b:b + 1, :], 0.0), axis=1, keepdims=True)
            m_old[:, cols] = 0.9 * (c1[:, cols].astype(F32) / 127.0 * sc1)
            v_old[:, cols] = 0.999 * ((c2[:, cols].astype(F32) / 255.0) ** 2 * sc2)

    def reduce_scatter(n1, n2, p1, p2, at1, at2, ring, fresh):
        rows = n2 * BLK
        half = n1 // 2
        pend = []

        def project(slot, d):
            block = ht[pl.ds(pl.multiple_of(d * rows, rows), rows), :]
            proj[slot, :rows, :] = jnp.dot(block, fac[...], preferred_element_type=F32)

        def lanes(g):
            return slice(g * LANES, (g + 1) * LANES)

        def hop(way, s, g, src):
            return pltpu.make_async_remote_copy(
                src_ref=src, dst_ref=ring.at[way * half + s, g],
                send_sem=send1.at[way, s, g], recv_sem=recv1.at[way, s, g],
                device_id=at1(1 if way == 0 else n1 - 1), device_id_type=MESH)

        def started(way, g):
            return (g < G // 2) == (way == 0)

        hops = {}
        project(0, (p1 + half) % n1)
        for g in range(G):
            way = 0 if g < G // 2 else 1
            fresh[way, g] = proj[0, :rows, lanes(g)].astype(BF16)
            c = hop(way, 0, g, fresh.at[way, g])
            c.start()
            hops[way, 0, g] = c
            pend.append(c)
        moments()
        for s in range(1, half):
            project(0, (p1 + half - s) % n1)
            project(1, (p1 + n1 - half + s) % n1)
            order = [g for g in range(G)]
            for i in range(G):
                for way in range(2):
                    g = order[i] if way == 0 else order[G - 1 - i]
                    val = proj[way, :rows, lanes(g)]
                    if s >= 2 or started(way, g):
                        hops[way, s - 1, g].wait_recv()
                        slot = ring.at[way * half + s - 1, g]
                        slot[...] = (val + slot[...].astype(F32)).astype(BF16)
                        c = hop(way, s, g, slot)
                    else:
                        fresh[way, g] = val.astype(BF16)
                        c = hop(way, s, g, fresh.at[way, g])
                    c.start()
                    hops[way, s, g] = c
                    pend.append(c)
        project(0, p1)
        for g in range(G):
            for way in range(2):
                hops[way, half - 1, g].wait_recv()
            val = (proj[0, :rows, lanes(g)] + ring[half - 1, g].astype(F32)) + ring[2 * half - 1, g].astype(F32)
            for j in range(n2):
                sumf[j * PACK + g * BLK:j * PACK + (g + 1) * BLK, :] = val[j * BLK:(j + 1) * BLK, :]
        msg[:n2] = sumf[:n2 * PACK, :].reshape(n2, PACK, LANES).astype(BF16)
        direct = []
        for k in far_first(n2):
            j = (p2 + k) % n2
            c = pltpu.make_async_remote_copy(
                src_ref=msg.at[j], dst_ref=land.at[k], send_sem=send2.at[k], recv_sem=recv2.at[k],
                device_id=at2(k), device_id_type=MESH)
            c.start()
            direct.append(c)
        total = sumf[pl.ds(pl.multiple_of(p2 * PACK, PACK), PACK), :]
        for i, k in reversed(list(enumerate(far_first(n2)))):
            direct[i].wait_recv()
            total = total + land[k].astype(F32)
        stack[...] = total
        for c in pend + direct:
            c.wait_send()

    @pl.when(core == 0)
    def _():
        reduce_scatter(NY, NZ, y, z, at_y, at_z, ring_y, fresh_y)

    @pl.when(core == 1)
    def _():
        reduce_scatter(NZ, NY, z, y, at_z, at_y, ring_z, fresh_z)

    for g in range(G):
        cols = slice(g * LANES, (g + 1) * LANES)
        low = stack[g * BLK:(g + 1) * BLK, :] / math.sqrt(tokens)
        first = m_old[:, cols] + 0.1 * low
        second = v_old[:, cols] + 0.001 * low * low
        m_ref[:, cols] = first
        v_ref[:, cols] = second
        norm[g * BLK:(g + 1) * BLK, :] = first / 0.19 / (jnp.sqrt(second / 0.001999) + 1e-8)
    gat[z] = norm[...].astype(BF16)

    pend = []
    for k in far_first(NZ):
        c = pltpu.make_async_remote_copy(
            src_ref=gat.at[z], dst_ref=gat.at[z], send_sem=send3.at[k], recv_sem=recv3.at[k],
            device_id=at_z(k), device_id_type=MESH)
        c.start()
        pend.append(c)
    for yy in range(NY):
        rows = pl.ds(pl.multiple_of((yy * NZ + z) * 64, 64), 64)
        bsel[yy * 64:(yy + 1) * 64, :] = bas[rows, :]
    for k in far_first(NZ)[::-1]:
        pltpu.make_async_remote_copy(
            src_ref=gat.at[z], dst_ref=gat.at[(z + NZ - k) % NZ], send_sem=send3.at[k], recv_sem=recv3.at[k],
            device_id=at_z(k), device_id_type=MESH).wait_recv()
    for zz in range(NZ):
        part = gat[zz].astype(F32)
        for g in range(G):
            rowsf[zz * BLK:(zz + 1) * BLK, g * LANES:(g + 1) * LANES] = part[g * BLK:(g + 1) * BLK, :]
    prod = lax.dot_general(bsel[...], rowsf[...].astype(BF16), (((1,), (1,)), ((), ())), preferred_element_type=F32)
    for yy in range(NY):
        wsend[yy] = prod[yy * 64:(yy + 1) * 64, :].astype(BF16)

    outs = []
    for k in far_first(NY):
        c = pltpu.make_async_remote_copy(
            src_ref=wsend.at[(y + k) % NY], dst_ref=wland.at[y], send_sem=send4.at[k], recv_sem=recv4.at[k],
            device_id=at_y(k), device_id_type=MESH)
        c.start()
        outs.append(c)
    wland[y] = wsend[y]
    for k in far_first(NY)[::-1]:
        pltpu.make_async_remote_copy(
            src_ref=wsend.at[y], dst_ref=wland.at[(y + NY - k) % NY], send_sem=send4.at[k], recv_sem=recv4.at[k],
            device_id=at_y(k), device_id_type=MESH).wait_recv()
    w_ref[...] = jnp.concatenate([wland[yy] for yy in range(NY)], axis=1)
    for c in pend + outs:
        c.wait_send()


def per_device(hidden_acts, out_grad, basis, code_first, scale_first, code_second, scale_second):
    tok, ff = hidden_acts.shape
    width = out_grad.shape[1]
    tokens = tok * lax.axis_size("dp")
    vm = pltpu.VMEM
    dma = pltpu.SemaphoreType.DMA
    any_spec = pl.BlockSpec(memory_space=pl.ANY)
    vmem_spec = pl.BlockSpec(memory_space=pltpu.VMEM)
    wt, first_new, second_new = pl.pallas_call(
        functools.partial(kernel, tokens=tokens),
        out_shape=(
            jax.ShapeDtypeStruct((64, ff), BF16),
            jax.ShapeDtypeStruct((BLK, RANK), F32),
            jax.ShapeDtypeStruct((BLK, RANK), F32),
        ),
        in_specs=[any_spec] * 7,
        out_specs=(vmem_spec,) * 3,
        scratch_shapes=[
            vm((tok, ff), BF16), vm((KC, tok, width // KC), BF16), vm((width, RANK), BF16),
            vm((BLK, RANK), jnp.int32), vm((2, BLK), F32), vm((BLK, RANK), jnp.int32), vm((2, BLK), F32),
            vm((ff, tok), F32), vm((NY * BLK, tok), F32), vm((ff, tok), BF16),
            vm((tok, RANK), F32), vm((tok, RANK), BF16), vm((2, NZ * BLK, RANK), F32),
            vm((BLK, RANK), F32), vm((BLK, RANK), F32),
            vm((NY, G, NZ * BLK, LANES), BF16), vm((NZ, G, NY * BLK, LANES), BF16),
            vm((2, G, NZ * BLK, LANES), BF16), vm((2, G, NY * BLK, LANES), BF16),
            vm((NZ * PACK, LANES), F32), vm((NZ, PACK, LANES), BF16), vm((NZ, PACK, LANES), BF16),
            vm((PACK, LANES), F32), vm((PACK, LANES), F32), vm((NZ, PACK, LANES), BF16),
            vm((NZ * BLK, RANK), F32), vm((NY * 64, RANK), BF16),
            vm((NY, 64, NZ * BLK), BF16), vm((NY, 64, NZ * BLK), BF16),
            dma((1 + 2 * KC + 4,)), dma((2, NZ // 2, G)), dma((2, NZ // 2, G)),
            dma((NZ,)), dma((NZ,)), dma((NZ,)), dma((NZ,)), dma((NY,)), dma((NY,)),
        ],
        compiler_params=pltpu.CompilerParams(
            collective_id=0, has_side_effects=True, vmem_limit_bytes=44 * 1024 * 1024),
    )(hidden_acts, out_grad, basis, code_first, scale_first.T, code_second, scale_second.T)
    return wt.T, first_new, second_new


def solution(mesh):
    state = P(("mp", "dp"), None)
    return jax.shard_map(
        per_device,
        mesh=mesh,
        in_specs=(P("dp", "mp"), P("dp", None), P(), state, state, state, state),
        out_specs=(P("mp", "dp"), state, state),
        check_vma=False,
    )
```

time: 410 us -> 71 us (0.17)
  waiting for transfers between devices: 376 us -> 0 us
  Pallas kernels: 0 us -> 60.7 us
  between operations: 14.8 us -> 0.66 us
  matrix products: 11.6 us -> 0 us
    unnamed x3 -> x0, waiting for transfers between devices: 253 us -> none
    all_gather x1 -> x0, waiting for transfers between devices: 122 us -> none  [per_device(): gathered = lax.all_gather(normalized, 'dp', axis=0, tiled=True)]
    pallas_call x0 -> x1, Pallas kernels: none -> 60.7 us  [per_device(): pl.pallas_call(functools.partial(kernel, tokens=tokens), out_shape=(jax.S...]
    dot_general x2 -> x0, matrix products: 11.6 us -> none  [the longest x1 9.29 us: per_device(): lax.dot_general(hidden_acts, factor, dims, preferred_element_type=jnp.flo...]
    unnamed x18 -> x15, local copies, waits for them, and re-layouts: 6.98 us -> 8.28 us
  transfers between devices with their start and end apart: 2 -> 0, of which waited for: 2 -> 0; matrix products, arithmetic and copies ran while one was open for 0% -> 0% of each run, Pallas kernels for 0% -> 0%
where the time goes in v1:
time: 71 us; the launch traced here: 69.6 us
  Pallas kernels  60.7 us (85%)
  local copies, waits for them, and re-layouts  8.28 us (12%)
    pallas_call x1, Pallas kernels, per_device(): pl.pallas_call(functools.partial(kernel, tokens=tokens), out_shape=(jax.S...  60.7 us
    unnamed x15, local copies, waits for them, and re-layouts  8.28 us

profile of v1, /device:TPU:6, one launch (start us, length us, event | category | flops | bytes accessed | tf_op | source)
XLA Modules:
  0.0 69.6 jit_solution(15703989439803291051)
XLA Ops:
  0.6 0.0 copy-start
  0.6 2.1 %copy-done = bf16[320,6144]{1,0:T(8,128)(2,1)S(1)} copy-done((bf16[320,6144]{1,0:T(8,128)(2,1)S(1)}, bf16[320,6144]{1,0:T(8,128)(2,1)}, u32[]{:S(2)}) %copy-start) | copy-done | bytes 3932184
  2.7 0.0 copy-start.1
  2.7 1.3 %copy-done.1 = bf16[320,1920]{1,0:T(8,128)(2,1)S(1)} copy-done((bf16[320,1920]{1,0:T(8,128)(2,1)S(1)}, bf16[320,1920]{1,0:T(8,128)(2,1)}, u32[]{:S(2)}) %copy-start.1) | copy-done | bytes 1228824
  4.0 0.0 copy-start.2
  4.0 0.8 %copy-done.2 = s32[20,512]{1,0:T(8,128)S(1)} copy-done((s32[20,512]{1,0:T(8,128)S(1)}, s32[20,512]{1,0:T(8,128)}, u32[]{:S(2)}) %copy-start.2) | copy-done | bytes 40984
  4.8 0.0 copy-start.3
  4.8 0.8 %copy-done.3 = s32[20,512]{1,0:T(8,128)S(1)} copy-done((s32[20,512]{1,0:T(8,128)S(1)}, s32[20,512]{1,0:T(8,128)}, u32[]{:S(2)}) %copy-start.3) | copy-done | bytes 40984
  5.6 0.0 copy-start.4
  5.6 0.7 copy-done.4
  6.3 0.0 copy-start.5
  6.3 0.7 copy-done.5
  7.0 60.7 %shard_map.94 = (bf16[64,1920]{1,0:T(8,128)(2,1)S(1)}, f32[20,512]{1,0:T(8,128)S(1)}, f32[20,512]{1,0:T(8,128)S(1)}) custom-call(bf16[320,1920]{1,0:T(8,128)(2,1)S(1)} %copy-done.1, bf16[320,6144]{1,0:T(8,128)(2,1)S(1)} %copy-done, bf16[6144,512]{1,0:T(8,128)(2,1)} %bas_hbm.1, s32[20,512]{1,0:T(8,128)S(1)} %copy-done.2, f32[2,20]{1,0:T(2,128)S(1)} %bitcast.4, ...), custom_call_target="tpu_custom_call" | custom-call | tf_op jit(solution)/shard_map/pallas_call | solution.py:248
  67.7 0.7 copy.13
  68.4 0.6 copy.14
  69.0 0.6 copy.15
Async XLA Ops:
  0.6 2.1 %copy-start = (bf16[320,6144]{1,0:T(8,128)(2,1)S(1)}, bf16[320,6144]{1,0:T(8,128)(2,1)}, u32[]{:S(2)}) copy-start(bf16[320,6144]{1,0:T(8,128)(2,1)} %og_hbm.1) | copy-start | bytes 11796484
  2.7 1.3 %copy-start.1 = (bf16[320,1920]{1,0:T(8,128)(2,1)S(1)}, bf16[320,1920]{1,0:T(8,128)(2,1)}, u32[]{:S(2)}) copy-start(bf16[320,1920]{1,0:T(8,128)(2,1)} %hid_hbm.1) | copy-start | bytes 3686404
  4.0 0.8 %copy-start.2 = (s32[20,512]{1,0:T(8,128)S(1)}, s32[20,512]{1,0:T(8,128)}, u32[]{:S(2)}) copy-start(s32[20,512]{1,0:T(8,128)} %c1_hbm.1) | copy-start | bytes 122884
  4.8 0.8 %copy-start.3 = (s32[20,512]{1,0:T(8,128)S(1)}, s32[20,512]{1,0:T(8,128)}, u32[]{:S(2)}) copy-start(s32[20,512]{1,0:T(8,128)} %c2_hbm.1) | copy-start | bytes 122884
  5.6 0.7 copy-start.4
  6.3 0.7 copy-start.5

commit v2 on v1

v2 whole, which is shorter than its diff:
```python
import functools
import math

import jax
import jax.numpy as jnp
from jax import lax
from jax.experimental import pallas as pl
from jax.experimental.pallas import tpu as pltpu
from jax.sharding import PartitionSpec as P

NY, NZ = 8, 12
BLK = 20
RANK = 512
LANES = 128
COLS = 64
G = RANK // LANES
PACK = G * BLK
KC = 4
F32, BF16 = jnp.float32, jnp.bfloat16
MESH = pl.DeviceIdType.MESH


def far_first(n):
    order = []
    for k in range(n // 2, 0, -1):
        order.append(k)
        if k != n - k:
            order.append(n - k)
    return order


def kernel(hid_hbm, og_hbm, bas_hbm, c1_hbm, s1_hbm, c2_hbm, s2_hbm,
           w_ref, m_ref, v_ref,
           hid, og, bas, c1, s1, c2, s2,
           htf, hperm, ht, acc, acc_other, fac, proj, m_old, v_old,
           land_y, land_z, fresh_y, fresh_z, sumf, msg, land,
           stack, norm, gat, rowsf, bsel, wsend_y, wland_y, wsend_z, wland_z, wide,
           load_sem, send0, recv0, send1, recv1, send2, recv2, send3, recv3, send4, recv4, *, tokens):
    dp, mp = lax.axis_index("dp"), lax.axis_index("mp")
    y, z = dp // NZ, dp % NZ
    core = mp % 2
    tok, ff = hid.shape
    kw = og.shape[2]

    def dev(yy, zz):
        return (yy * NZ + zz, mp)

    def at_y(k):
        return dev((y + k) % NY, z)

    def at_z(k):
        return dev(y, (z + k) % NZ)

    loads = []
    base = core * (KC * kw)
    for k in range(KC):
        at = pl.ds(pl.multiple_of(base + k * kw, kw), kw)
        loads.append(pltpu.make_async_copy(og_hbm.at[:, at], og.at[k], load_sem.at[k]))
        loads.append(pltpu.make_async_copy(bas_hbm.at[at], bas.at[pl.ds(k * kw, kw)], load_sem.at[KC + k]))
    load_hid = pltpu.make_async_copy(hid_hbm, hid, load_sem.at[2 * KC])
    small = [(c1_hbm, c1), (s1_hbm, s1), (c2_hbm, c2), (s2_hbm, s2)]
    small = [pltpu.make_async_copy(a, b, load_sem.at[1 + 2 * KC + i]) for i, (a, b) in enumerate(small)]
    for c in loads + [load_hid] + small:
        c.start()

    barrier = pltpu.get_barrier_semaphore()
    for k in range(1, NY):
        pl.semaphore_signal(barrier, inc=1, device_id=at_y(k), device_id_type=MESH)
    for k in range(1, NZ):
        pl.semaphore_signal(barrier, inc=1, device_id=at_z(k), device_id_type=MESH)

    pl.semaphore_signal(barrier, inc=1, device_id=(dp, mp + 1 - 2 * core), device_id_type=MESH)

    swaps = []
    width = RANK // 2
    for k in range(KC):
        loads[2 * k].wait()
        loads[2 * k + 1].wait()
        for h in range(2):
            part = jnp.dot(og[k], bas[k * kw:(k + 1) * kw, h * width:(h + 1) * width], preferred_element_type=F32)
            acc[h] = part if k == 0 else acc[h] + part
            if k == KC - 1:
                if h == 0:
                    pl.semaphore_wait(barrier, NY - 1 + NZ - 1 + 1)
                c = pltpu.make_async_remote_copy(
                    src_ref=acc.at[h], dst_ref=acc_other.at[h], send_sem=send0.at[h], recv_sem=recv0.at[h],
                    device_id=(dp, mp + 1 - 2 * core), device_id_type=MESH)
                c.start()
                swaps.append(c)

    load_hid.wait()
    for c in range(ff // LANES):
        htf[c * LANES:(c + 1) * LANES, :] = hid[:, c * LANES:(c + 1) * LANES].astype(F32).T

    @pl.when(core == 0)
    def _():
        ht[...] = htf[...].astype(BF16)

    @pl.when(core == 1)
    def _():
        for zz in range(NZ):
            for yy in range(NY):
                at = yy * NZ * BLK + zz * BLK
                hperm[yy * BLK:(yy + 1) * BLK, :] = htf[at:at + BLK, :]
            ht[zz * NY * BLK:(zz + 1) * NY * BLK, :] = hperm[...].astype(BF16)

    for h in range(2):
        swaps[h].wait_recv()
        fac[:, h * width:(h + 1) * width] = (acc[h] + acc_other[h]).astype(BF16)

    late = []
    for yy in range(NY):
        late.append(pltpu.make_async_copy(
            bas_hbm.at[pl.ds(pl.multiple_of((yy * NZ + z) * COLS, COLS), COLS)],
            bsel.at[pl.ds(yy * COLS, COLS)], load_sem.at[2 * KC + 5 + yy]))
    late_z = pltpu.make_async_copy(
        bas_hbm.at[pl.ds(pl.multiple_of(y * NZ * COLS, COLS), NZ * COLS)], bsel, load_sem.at[2 * KC + 5])

    @pl.when(core == 0)
    def _():
        for c in late:
            c.start()

    @pl.when(core == 1)
    def _():
        late_z.start()

    def moments():
        for c in small:
            c.wait()
        eye = lax.broadcasted_iota(jnp.int32, (BLK, BLK), 0) == lax.broadcasted_iota(jnp.int32, (BLK, BLK), 1)
        half = RANK // 2
        for b in range(2):
            cols = slice(b * half, (b + 1) * half)
            sc1 = jnp.sum(jnp.where(eye, s1[b:b + 1, :], 0.0), axis=1, keepdims=True)
            sc2 = jnp.sum(jnp.where(eye, s2[b:b + 1, :], 0.0), axis=1, keepdims=True)
            m_old[:, cols] = 0.9 * (c1[:, cols].astype(F32) / 127.0 * sc1)
            v_old[:, cols] = 0.999 * ((c2[:, cols].astype(F32) / 255.0) ** 2 * sc2)

    def lanes(g):
        return slice(g * LANES, (g + 1) * LANES)

    def near(way, g):
        return (g < G // 2) == (way == 0)

    def project(slot, d, rows):
        block = ht[pl.ds(pl.multiple_of(d * rows, rows), rows), :]
        proj[slot, :rows, :] = jnp.dot(block, fac[...], preferred_element_type=F32)

    def ring_sum(rows):
        half = NY // 2
        pend, hops = [], {}

        def hop(way, s, g, src):
            c = pltpu.make_async_remote_copy(
                src_ref=src, dst_ref=land_y.at[way * half + s, g],
                send_sem=send1.at[way, s, g], recv_sem=recv1.at[way, s, g],
                device_id=at_y(1 if way == 0 else NY - 1), device_id_type=MESH)
            c.start()
            hops[way, s, g] = c
            pend.append(c)

        project(0, (y + half) % NY, rows)
        for g in range(G):
            way = 0 if near(0, g) else 1
            fresh_y[way, g] = proj[0, :rows, lanes(g)].astype(BF16)
            hop(way, 0, g, fresh_y.at[way, g])
        moments()
        for s in range(1, half):
            project(0, (y + half - s) % NY, rows)
            project(1, (y + half + s) % NY, rows)
            for i in range(G):
                for way in range(2):
                    g = i if way == 0 else G - 1 - i
                    val = proj[way, :rows, lanes(g)]
                    if s >= 2 or near(way, g):
                        hops[way, s - 1, g].wait_recv()
                        slot = land_y.at[way * half + s - 1, g]
                        slot[...] = (val + slot[...].astype(F32)).astype(BF16)
                        hop(way, s, g, slot)
                    else:
                        fresh_y[way, g] = val.astype(BF16)
                        hop(way, s, g, fresh_y.at[way, g])
        project(0, y, rows)
        for g in range(G):
            val = proj[0, :rows, lanes(g)]
            for way in range(2):
                hops[way, half - 1, g].wait_recv()
                val = val + land_y[way * half + half - 1, g].astype(F32)
            stacked(g, val, NZ)
        return pend

    def tree_sum(rows):
        pend, hops = [], {}

        def send(way, d, step, g, val):
            fresh_z[way, d - 1, g] = val.astype(BF16)
            c = pltpu.make_async_remote_copy(
                src_ref=fresh_z.at[way, d - 1, g], dst_ref=land_z.at[way, d - 1, g],
                send_sem=send1.at[way, d - 1, g], recv_sem=recv1.at[way, d - 1, g],
                device_id=at_z(step if way == 0 else NZ - step), device_id_type=MESH)
            c.start()
            hops[way, d, g] = c
            pend.append(c)

        def got(way, d, g):
            hops[way, d, g].wait_recv()
            return land_z[way, d - 1, g].astype(F32)

        def chunk(d):
            project(0, (z + d) % NZ, rows)
            project(1, (z + NZ - d) % NZ, rows)

        def leaf(d):
            chunk(d)
            for i in range(G):
                for way in range(2):
                    g = i if way == 0 else G - 1 - i
                    send(way, d, 1, g, proj[way, :rows, lanes(g)])

        def inner(d):
            chunk(d)
            for i in range(G):
                for way in range(2):
                    g = i if way == 0 else G - 1 - i
                    val = proj[way, :rows, lanes(g)] + got(way, d + 1, g)
                    if d + 2 < NZ // 2 or near(way, g):
                        val = val + got(way, d + 2, g)
                    send(way, d, 2, g, val)

        project(0, (z + NZ // 2) % NZ, rows)
        for g in (0, G - 1) + tuple(range(1, G - 1)):
            send(0 if near(0, g) else 1, NZ // 2, 2, g, proj[0, :rows, lanes(g)])
        leaf(5)
        leaf(3)
        moments()
        inner(4)
        leaf(1)
        inner(2)
        project(0, z, rows)
        for g in range(G):
            val = proj[0, :rows, lanes(g)]
            for d in (1, 2):
                for way in range(2):
                    val = val + got(way, d, g)
            stacked(g, val, NY)
        return pend

    def stacked(g, val, n2):
        for j in range(n2):
            sumf[j * PACK + g * BLK:j * PACK + (g + 1) * BLK, :] = val[j * BLK:(j + 1) * BLK, :]

    def direct_sum(n2, p2, at2, pend):
        msg[:n2] = sumf[:n2 * PACK, :].reshape(n2, PACK, LANES).astype(BF16)
        direct = []
        for k in far_first(n2):
            j = (p2 + k) % n2
            c = pltpu.make_async_remote_copy(
                src_ref=msg.at[j], dst_ref=land.at[k], send_sem=send2.at[k], recv_sem=recv2.at[k],
                device_id=at2(k), device_id_type=MESH)
            c.start()
            direct.append(c)
        total = sumf[pl.ds(pl.multiple_of(p2 * PACK, PACK), PACK), :]
        for i, k in reversed(list(enumerate(far_first(n2)))):
            direct[i].wait_recv()
            total = total + land[k].astype(F32)
        stack[...] = total
        for c in pend + direct:
            c.wait_send()

    @pl.when(core == 0)
    def _():
        direct_sum(NZ, z, at_z, ring_sum(NZ * BLK))

    @pl.when(core == 1)
    def _():
        direct_sum(NY, y, at_y, tree_sum(NY * BLK))

    for g in range(G):
        cols = slice(g * LANES, (g + 1) * LANES)
        low = stack[g * BLK:(g + 1) * BLK, :] / math.sqrt(tokens)
        first = m_old[:, cols] + 0.1 * low
        second = v_old[:, cols] + 0.001 * low * low
        m_ref[:, cols] = first
        v_ref[:, cols] = second
        norm[g * BLK:(g + 1) * BLK, :] = first / 0.19 / (jnp.sqrt(second / 0.001999) + 1e-8)

    def gather(n, p, at):
        gat[p] = norm[...].astype(BF16)
        sends = []
        for k in far_first(n):
            c = pltpu.make_async_remote_copy(
                src_ref=gat.at[p], dst_ref=gat.at[p], send_sem=send3.at[k], recv_sem=recv3.at[k],
                device_id=at(k), device_id_type=MESH)
            c.start()
            sends.append(c)
        for k in far_first(n)[::-1]:
            pltpu.make_async_remote_copy(
                src_ref=gat.at[p], dst_ref=gat.at[(p + n - k) % n], send_sem=send3.at[k], recv_sem=recv3.at[k],
                device_id=at(k), device_id_type=MESH).wait_recv()
        for b in range(n):
            part = gat[b].astype(F32)
            for g in range(G):
                rowsf[b * BLK:(b + 1) * BLK, g * LANES:(g + 1) * LANES] = part[g * BLK:(g + 1) * BLK, :]
        return sends

    def exchange(n, p, at, src, dst):
        sends = []
        for k in far_first(n):
            c = pltpu.make_async_remote_copy(
                src_ref=src.at[(p + k) % n], dst_ref=dst.at[p], send_sem=send4.at[k], recv_sem=recv4.at[k],
                device_id=at(k), device_id_type=MESH)
            c.start()
            sends.append(c)
        dst[p] = src[p]
        for k in far_first(n)[::-1]:
            pltpu.make_async_remote_copy(
                src_ref=src.at[p], dst_ref=dst.at[(p + n - k) % n], send_sem=send4.at[k], recv_sem=recv4.at[k],
                device_id=at(k), device_id_type=MESH).wait_recv()
        return sends

    nt = (((1,), (1,)), ((), ()))

    @pl.when(core == 0)
    def _():
        sends = gather(NZ, z, at_z)
        for c in late:
            c.wait()
        prod = lax.dot_general(bsel[:NY * COLS, :], rowsf[...].astype(BF16), nt, preferred_element_type=F32)
        for yy in range(NY):
            wsend_y[yy] = prod[yy * COLS:(yy + 1) * COLS, :].astype(BF16)
        sends += exchange(NY, y, at_y, wsend_y, wland_y)
        w_ref[...] = jnp.concatenate([wland_y[yy] for yy in range(NY)], axis=1)
        for c in sends:
            c.wait_send()

    @pl.when(core == 1)
    def _():
        sends = gather(NY, y, at_y)
        late_z.wait()
        part = NY // 2 * BLK
        rows = rowsf[:NY * BLK, :].astype(BF16)
        left = lax.broadcasted_iota(jnp.int32, (part, LANES), 1) < COLS
        for q in range(NZ // 2):
            pair = lax.dot_general(rows, bsel[q * LANES:(q + 1) * LANES, :], nt, preferred_element_type=F32)
            low, high = pair[:part, :], pair[part:, :]
            wsend_z[2 * q] = jnp.where(left, low, pltpu.roll(high, COLS, 1)).astype(BF16)
            wsend_z[2 * q + 1] = jnp.where(left, pltpu.roll(low, COLS, 1), high).astype(BF16)
        sends += exchange(NZ, z, at_z, wsend_z, wland_z)
        for zz in range(NZ):
            got = wland_z[zz].astype(F32)
            for b in range(NY // 2):
                at = b * NZ * BLK + zz * BLK
                wide[at:at + BLK, :] = got[b * BLK:(b + 1) * BLK, :]
        wt = wide[...].T.astype(BF16)
        w_ref[...] = jnp.concatenate([wt[:COLS, :], wt[COLS:, :]], axis=1)
        for c in sends:
            c.wait_send()

    for c in swaps:
        c.wait_send()


def per_device(hidden_acts, out_grad, basis, code_first, scale_first, code_second, scale_second):
    tok, ff = hidden_acts.shape
    width = out_grad.shape[1]
    tokens = tok * lax.axis_size("dp")
    vm = pltpu.VMEM
    dma = pltpu.SemaphoreType.DMA
    any_spec = pl.BlockSpec(memory_space=pl.ANY)
    vmem_spec = pl.BlockSpec(memory_space=pltpu.VMEM)
    wt, first_new, second_new = pl.pallas_call(
        functools.partial(kernel, tokens=tokens),
        out_shape=(
            jax.ShapeDtypeStruct((COLS, ff), BF16),
            jax.ShapeDtypeStruct((BLK, RANK), F32),
            jax.ShapeDtypeStruct((BLK, RANK), F32),
        ),
        in_specs=[any_spec] * 7,
        out_specs=(vmem_spec,) * 3,
        scratch_shapes=[
            vm((tok, ff), BF16), vm((KC, tok, width // 2 // KC), BF16), vm((width // 2, RANK), BF16),
            vm((BLK, RANK), jnp.int32), vm((2, BLK), F32), vm((BLK, RANK), jnp.int32), vm((2, BLK), F32),
            vm((ff, tok), F32), vm((NY * BLK, tok), F32), vm((ff, tok), BF16),
            vm((2, tok, RANK // 2), F32), vm((2, tok, RANK // 2), F32), vm((tok, RANK), BF16), vm((2, NZ * BLK, RANK), F32),
            vm((BLK, RANK), F32), vm((BLK, RANK), F32),
            vm((NY, G, NZ * BLK, LANES), BF16), vm((2, NZ // 2, G, NY * BLK, LANES), BF16),
            vm((2, G, NZ * BLK, LANES), BF16), vm((2, NZ // 2, G, NY * BLK, LANES), BF16),
            vm((NZ * PACK, LANES), F32), vm((NZ, PACK, LANES), BF16), vm((NZ, PACK, LANES), BF16),
            vm((PACK, LANES), F32), vm((PACK, LANES), F32), vm((NZ, PACK, LANES), BF16),
            vm((NZ * BLK, RANK), F32), vm((NZ * COLS, RANK), BF16),
            vm((NY, COLS, NZ * BLK), BF16), vm((NY, COLS, NZ * BLK), BF16),
            vm((NZ, PACK, LANES), BF16), vm((NZ, PACK, LANES), BF16), vm((ff // 2, LANES), F32),
            dma((2 * KC + 5 + NY,)), dma((2,)), dma((2,)), dma((2, NZ // 2, G)), dma((2, NZ // 2, G)),
            dma((NZ,)), dma((NZ,)), dma((NZ,)), dma((NZ,)), dma((NZ,)), dma((NZ,)),
        ],
        compiler_params=pltpu.CompilerParams(
            collective_id=0, has_side_effects=True, vmem_limit_bytes=44 * 1024 * 1024),
    )(*[pltpu.with_memory_space_constraint(a, pltpu.HBM) for a in (hidden_acts, out_grad, basis, code_first, scale_first.T, code_second, scale_second.T)])
    return wt.T, first_new, second_new


def solution(mesh):
    state = P(("mp", "dp"), None)
    return jax.shard_map(
        per_device,
        mesh=mesh,
        in_specs=(P("dp", "mp"), P("dp", None), P(), state, state, state, state),
        out_specs=(P("mp", "dp"), state, state),
        check_vma=False,
    )
```

time: 71 us -> 65.5 us (0.923); the launches traced: 69.6 us -> 65.1 us
  local copies, waits for them, and re-layouts: 8.28 us -> 1.93 us
  Pallas kernels: 60.7 us -> 62.5 us
    unnamed x15 -> x3, local copies, waits for them, and re-layouts: 8.28 us -> 1.93 us
    pallas_call x1, Pallas kernels: 60.7 us -> 62.5 us  [per_device(): pl.pallas_call(functools.partial(kernel, tokens=tokens), out_shape=(jax.S...]
where the time goes in v2:
time: 65.5 us; the launch traced here: 65.1 us
  Pallas kernels  62.5 us (95%)
  local copies, waits for them, and re-layouts  1.93 us (3%)
    pallas_call x1, Pallas kernels, per_device(): pl.pallas_call(functools.partial(kernel, tokens=tokens), out_shape=(jax.S...  62.5 us
    unnamed x3, local copies, waits for them, and re-layouts  1.93 us

profile of v2, /device:TPU:6, one launch (start us, length us, event | category | flops | bytes accessed | tf_op | source)
XLA Modules:
  0.0 65.1 jit_solution(12796034345551015487)
XLA Ops:
  0.6 62.5 %shard_map.94 = (bf16[64,1920]{1,0:T(8,128)(2,1)S(1)}, f32[20,512]{1,0:T(8,128)S(1)}, f32[20,512]{1,0:T(8,128)S(1)}) custom-call(bf16[320,1920]{1,0:T(8,128)(2,1)} %hid_hbm.1, bf16[320,6144]{1,0:T(8,128)(2,1)} %og_hbm.1, bf16[6144,512]{1,0:T(8,128)(2,1)} %bas_hbm.1, s32[20,512]{1,0:T(8,128)} %c1_hbm.1, f32[2,20]{1,0:T(2,128)} %bitcast.4, s32[20,512]{1,0:T(8,128)} %c2_hbm.1, ...), custom_call_target="tpu_custom_call" | custom-call | tf_op jit(solution)/shard_map/pallas_call | solution.py:372
  63.1 0.7 %copy.13 = bf16[1920,64]{0,1:T(8,128)(2,1)} copy(bf16[1920,64]{0,1:T(8,128)(2,1)S(1)} %bitcast.3) | data formatting | bytes 491520
  63.8 0.6 copy.14
  64.4 0.6 copy.15

commit v3 on v2

--- a/solution.py
+++ b/solution.py
@@ -265,25 +265,17 @@
             direct[i].wait_recv()
             total = total + land[k].astype(F32)
         stack[...] = total
-        for c in pend + direct:
-            c.wait_send()
-
-    @pl.when(core == 0)
-    def _():
-        direct_sum(NZ, z, at_z, ring_sum(NZ * BLK))
-
-    @pl.when(core == 1)
-    def _():
-        direct_sum(NY, y, at_y, tree_sum(NY * BLK))
-
-    for g in range(G):
-        cols = slice(g * LANES, (g + 1) * LANES)
-        low = stack[g * BLK:(g + 1) * BLK, :] / math.sqrt(tokens)
-        first = m_old[:, cols] + 0.1 * low
-        second = v_old[:, cols] + 0.001 * low * low
-        m_ref[:, cols] = first
-        v_ref[:, cols] = second
-        norm[g * BLK:(g + 1) * BLK, :] = first / 0.19 / (jnp.sqrt(second / 0.001999) + 1e-8)
+        return pend + direct
+
+    def adam():
+        for g in range(G):
+            cols = slice(g * LANES, (g + 1) * LANES)
+            low = stack[g * BLK:(g + 1) * BLK, :] / math.sqrt(tokens)
+            first = m_old[:, cols] + 0.1 * low
+            second = v_old[:, cols] + 0.001 * low * low
+            m_ref[:, cols] = first
+            v_ref[:, cols] = second
+            norm[g * BLK:(g + 1) * BLK, :] = first / 0.19 / (jnp.sqrt(second / 0.001999) + 1e-8)
 
     def gather(n, p, at):
         gat[p] = norm[...].astype(BF16)
@@ -323,7 +315,9 @@
 
     @pl.when(core == 0)
     def _():
-        sends = gather(NZ, z, at_z)
+        sends = direct_sum(NZ, z, at_z, ring_sum(NZ * BLK))
+        adam()
+        sends += gather(NZ, z, at_z)
         for c in late:
             c.wait()
         prod = lax.dot_general(bsel[:NY * COLS, :], rowsf[...].astype(BF16), nt, preferred_element_type=F32)
@@ -336,7 +330,9 @@
 
     @pl.when(core == 1)
     def _():
-        sends = gather(NY, y, at_y)
+        sends = direct_sum(NY, y, at_y, tree_sum(NY * BLK))
+        adam()
+        sends += gather(NY, y, at_y)
         late_z.wait()
         part = NY // 2 * BLK
         rows = rowsf[:NY * BLK, :].astype(BF16)
@@ -359,6 +355,15 @@
 
     for c in swaps:
         c.wait_send()
+
+
+def store(wt, first_new, second_new, wt_out, first_out, second_out, sem):
+    pairs = ((wt, wt_out), (first_new, first_out), (second_new, second_out))
+    copies = [pltpu.make_async_copy(a, b, sem.at[i]) for i, (a, b) in enumerate(pairs)]
+    for c in copies:
+        c.start()
+    for c in copies:
+        c.wait()
 
 
 def per_device(hidden_acts, out_grad, basis, code_first, scale_first, code_second, scale_second):
@@ -397,6 +402,14 @@
         compiler_params=pltpu.CompilerParams(
             collective_id=0, has_side_effects=True, vmem_limit_bytes=44 * 1024 * 1024),
     )(*[pltpu.with_memory_space_constraint(a, pltpu.HBM) for a in (hidden_acts, out_grad, basis, code_first, scale_first.T, code_second, scale_second.T)])
+    wt, first_new, second_new = pl.pallas_call(
+        store,
+        out_shape=[jax.ShapeDtypeStruct(a.shape, a.dtype) for a in (wt, first_new, second_new)],
+        in_specs=[any_spec] * 3,
+        out_specs=[any_spec] * 3,
+        scratch_shapes=[dma((3,))],
+        compiler_params=pltpu.CompilerParams(vmem_limit_bytes=1024 * 1024),
+    )(wt, first_new, second_new)
     return wt.T, first_new, second_new
 
 

time: 65.5 us -> 64.7 us (0.988)
  local copies, waits for them, and re-layouts: 1.93 us -> 0 us
  Pallas kernels: 62.5 us -> 63.2 us
    unnamed x3 -> x0, local copies, waits for them, and re-layouts: 1.93 us -> none
    pallas_call x0 -> x1, Pallas kernels: none -> 0.75 us  [per_device(): pl.pallas_call(store, out_shape=[jax.ShapeDtypeStruct(a.shape, a.dtype) f...]
where the time goes in v3:
time: 64.7 us; the launch traced here: 63.9 us
  Pallas kernels  63.2 us (98%)
    pallas_call x1, Pallas kernels, per_device(): pl.pallas_call(functools.partial(kernel, tokens=tokens), out_shape=(jax.S...  62.5 us

profile of v3, /device:TPU:6, one launch (start us, length us, event | category | flops | bytes accessed | tf_op | source)
XLA Modules:
  0.0 63.9 jit_solution(1180014555572230353)
XLA Ops:
  0.6 62.5 %shard_map.94 = (bf16[64,1920]{1,0:T(8,128)(2,1)S(1)}, f32[20,512]{1,0:T(8,128)S(1)}, f32[20,512]{1,0:T(8,128)S(1)}) custom-call(bf16[320,1920]{1,0:T(8,128)(2,1)} %hid_hbm.1, bf16[320,6144]{1,0:T(8,128)(2,1)} %og_hbm.1, bf16[6144,512]{1,0:T(8,128)(2,1)} %bas_hbm.1, s32[20,512]{1,0:T(8,128)} %c1_hbm.1, f32[2,20]{1,0:T(2,128)} %bitcast.3, s32[20,512]{1,0:T(8,128)} %c2_hbm.1, ...), custom_call_target="tpu_custom_call" | custom-call | tf_op jit(solution)/shard_map/pallas_call | solution.py:377
  63.1 0.7 %shard_map.95 = (bf16[64,1920]{1,0:T(8,128)(2,1)}, f32[20,512]{1,0:T(8,128)}, f32[20,512]{1,0:T(8,128)}) custom-call(bf16[64,1920]{1,0:T(8,128)(2,1)S(1)} %get-tuple-element.9.wt, f32[20,512]{1,0:T(8,128)S(1)} %get-tuple-element.10.first_new, f32[20,512]{1,0:T(8,128)S(1)} %get-tuple-element.11.second_new), custom_call_target="tpu_custom_call" | custom-call | tf_op jit(solution)/shard_map/pallas_call | solution.py:405

commit v4 on v3

--- a/solution.py
+++ b/solution.py
@@ -60,20 +60,42 @@
     load_hid = pltpu.make_async_copy(hid_hbm, hid, load_sem.at[2 * KC])
     small = [(c1_hbm, c1), (s1_hbm, s1), (c2_hbm, c2), (s2_hbm, s2)]
     small = [pltpu.make_async_copy(a, b, load_sem.at[1 + 2 * KC + i]) for i, (a, b) in enumerate(small)]
-    for c in loads + [load_hid] + small:
+    for c in loads[:-2] + [load_hid] + loads[-2:]:
         c.start()
 
     barrier = pltpu.get_barrier_semaphore()
-    for k in range(1, NY):
+    for k in far_first(NY):
         pl.semaphore_signal(barrier, inc=1, device_id=at_y(k), device_id_type=MESH)
-    for k in range(1, NZ):
+    for k in far_first(NZ):
         pl.semaphore_signal(barrier, inc=1, device_id=at_z(k), device_id_type=MESH)
 
     pl.semaphore_signal(barrier, inc=1, device_id=(dp, mp + 1 - 2 * core), device_id_type=MESH)
+
+    for c in small:
+        c.start()
+
+    def transpose_hidden():
+        load_hid.wait()
+        for c in range(ff // LANES):
+            htf[c * LANES:(c + 1) * LANES, :] = hid[:, c * LANES:(c + 1) * LANES].astype(F32).T
+
+        @pl.when(core == 0)
+        def _():
+            ht[...] = htf[...].astype(BF16)
+
+        @pl.when(core == 1)
+        def _():
+            for zz in range(NZ):
+                for yy in range(NY):
+                    at = yy * NZ * BLK + zz * BLK
+                    hperm[yy * BLK:(yy + 1) * BLK, :] = htf[at:at + BLK, :]
+                ht[zz * NY * BLK:(zz + 1) * NY * BLK, :] = hperm[...].astype(BF16)
 
     swaps = []
     width = RANK // 2
     for k in range(KC):
+        if k == KC - 1:
+            transpose_hidden()
         loads[2 * k].wait()
         loads[2 * k + 1].wait()
         for h in range(2):
@@ -88,22 +110,6 @@
                 c.start()
                 swaps.append(c)
 
-    load_hid.wait()
-    for c in range(ff // LANES):
-        htf[c * LANES:(c + 1) * LANES, :] = hid[:, c * LANES:(c + 1) * LANES].astype(F32).T
-
-    @pl.when(core == 0)
-    def _():
-        ht[...] = htf[...].astype(BF16)
-
-    @pl.when(core == 1)
-    def _():
-        for zz in range(NZ):
-            for yy in range(NY):
-                at = yy * NZ * BLK + zz * BLK
-                hperm[yy * BLK:(yy + 1) * BLK, :] = htf[at:at + BLK, :]
-            ht[zz * NY * BLK:(zz + 1) * NY * BLK, :] = hperm[...].astype(BF16)
-
     for h in range(2):
         swaps[h].wait_recv()
         fac[:, h * width:(h + 1) * width] = (acc[h] + acc_other[h]).astype(BF16)
@@ -147,69 +153,26 @@
         block = ht[pl.ds(pl.multiple_of(d * rows, rows), rows), :]
         proj[slot, :rows, :] = jnp.dot(block, fac[...], preferred_element_type=F32)
 
-    def ring_sum(rows):
-        half = NY // 2
+    def tree_sum(n, p, at, fresh, land, rows, n2, plan):
         pend, hops = [], {}
 
-        def hop(way, s, g, src):
+        def send(way, d, step, g, val):
+            fresh[way, d - 1, g] = val.astype(BF16)
             c = pltpu.make_async_remote_copy(
-                src_ref=src, dst_ref=land_y.at[way * half + s, g],
-                send_sem=send1.at[way, s, g], recv_sem=recv1.at[way, s, g],
-                device_id=at_y(1 if way == 0 else NY - 1), device_id_type=MESH)
-            c.start()
-            hops[way, s, g] = c
-            pend.append(c)
-
-        project(0, (y + half) % NY, rows)
-        for g in range(G):
-            way = 0 if near(0, g) else 1
-            fresh_y[way, g] = proj[0, :rows, lanes(g)].astype(BF16)
-            hop(way, 0, g, fresh_y.at[way, g])
-        moments()
-        for s in range(1, half):
-            project(0, (y + half - s) % NY, rows)
-            project(1, (y + half + s) % NY, rows)
-            for i in range(G):
-                for way in range(2):
-                    g = i if way == 0 else G - 1 - i
-                    val = proj[way, :rows, lanes(g)]
-                    if s >= 2 or near(way, g):
-                        hops[way, s - 1, g].wait_recv()
-                        slot = land_y.at[way * half + s - 1, g]
-                        slot[...] = (val + slot[...].astype(F32)).astype(BF16)
-                        hop(way, s, g, slot)
-                    else:
-                        fresh_y[way, g] = val.astype(BF16)
-                        hop(way, s, g, fresh_y.at[way, g])
-        project(0, y, rows)
-        for g in range(G):
-            val = proj[0, :rows, lanes(g)]
-            for way in range(2):
-                hops[way, half - 1, g].wait_recv()
-                val = val + land_y[way * half + half - 1, g].astype(F32)
-            stacked(g, val, NZ)
-        return pend
-
-    def tree_sum(rows):
-        pend, hops = [], {}
-
-        def send(way, d, step, g, val):
-            fresh_z[way, d - 1, g] = val.astype(BF16)
-            c = pltpu.make_async_remote_copy(
-                src_ref=fresh_z.at[way, d - 1, g], dst_ref=land_z.at[way, d - 1, g],
+                src_ref=fresh.at[way, d - 1, g], dst_ref=land.at[way, d - 1, g],
                 send_sem=send1.at[way, d - 1, g], recv_sem=recv1.at[way, d - 1, g],
-                device_id=at_z(step if way == 0 else NZ - step), device_id_type=MESH)
+                device_id=at(step if way == 0 else n - step), device_id_type=MESH)
             c.start()
             hops[way, d, g] = c
             pend.append(c)
 
         def got(way, d, g):
             hops[way, d, g].wait_recv()
-            return land_z[way, d - 1, g].astype(F32)
+            return land[way, d - 1, g].astype(F32)
 
         def chunk(d):
-            project(0, (z + d) % NZ, rows)
-            project(1, (z + NZ - d) % NZ, rows)
+            project(0, (p + d) % n, rows)
+            project(1, (p + n - d) % n, rows)
 
         def leaf(d):
             chunk(d)
@@ -218,32 +181,33 @@
                     g = i if way == 0 else G - 1 - i
                     send(way, d, 1, g, proj[way, :rows, lanes(g)])
 
-        def inner(d):
+        def inner(d, sources, step):
             chunk(d)
             for i in range(G):
                 for way in range(2):
                     g = i if way == 0 else G - 1 - i
-                    val = proj[way, :rows, lanes(g)] + got(way, d + 1, g)
-                    if d + 2 < NZ // 2 or near(way, g):
-                        val = val + got(way, d + 2, g)
-                    send(way, d, 2, g, val)
-
-        project(0, (z + NZ // 2) % NZ, rows)
+                    val = proj[way, :rows, lanes(g)]
+                    for far in sources:
+                        if far < n // 2 or near(way, g):
+                            val = val + got(way, far, g)
+                    send(way, d, step, g, val)
+
+        project(0, (p + n // 2) % n, rows)
         for g in (0, G - 1) + tuple(range(1, G - 1)):
-            send(0 if near(0, g) else 1, NZ // 2, 2, g, proj[0, :rows, lanes(g)])
-        leaf(5)
-        leaf(3)
-        moments()
-        inner(4)
-        leaf(1)
-        inner(2)
-        project(0, z, rows)
+            send(0 if near(0, g) else 1, n // 2, 2, g, proj[0, :rows, lanes(g)])
+        for at_step, (d, sources, step) in enumerate(plan):
+            if at_step == 1:
+                moments()
+            if sources:
+                inner(d, sources, step)
+            else:
+                leaf(d)
+        project(0, p, rows)
         for g in range(G):
             val = proj[0, :rows, lanes(g)]
-            for d in (1, 2):
-                for way in range(2):
-                    val = val + got(way, d, g)
-            stacked(g, val, NY)
+            for way in range(2):
+                val = val + got(way, 1, g)
+            stacked(g, val, n2)
         return pend
 
     def stacked(g, val, n2):
@@ -315,7 +279,8 @@
 
     @pl.when(core == 0)
     def _():
-        sends = direct_sum(NZ, z, at_z, ring_sum(NZ * BLK))
+        sends = direct_sum(NZ, z, at_z, tree_sum(
+            NY, y, at_y, fresh_y, land_y, NZ * BLK, NZ, ((3, (), 1), (2, (3, 4), 1), (1, (2,), 1))))
         adam()
         sends += gather(NZ, z, at_z)
         for c in late:
@@ -330,7 +295,9 @@
 
     @pl.when(core == 1)
     def _():
-        sends = direct_sum(NY, y, at_y, tree_sum(NY * BLK))
+        sends = direct_sum(NY, y, at_y, tree_sum(
+            NZ, z, at_z, fresh_z, land_z, NY * BLK, NY,
+            ((5, (), 1), (3, (), 1), (4, (5, 6), 2), (2, (3, 4), 1), (1, (2,), 1))))
         adam()
         sends += gather(NY, y, at_y)
         late_z.wait()
@@ -389,8 +356,8 @@
             vm((ff, tok), F32), vm((NY * BLK, tok), F32), vm((ff, tok), BF16),
             vm((2, tok, RANK // 2), F32), vm((2, tok, RANK // 2), F32), vm((tok, RANK), BF16), vm((2, NZ * BLK, RANK), F32),
             vm((BLK, RANK), F32), vm((BLK, RANK), F32),
-            vm((NY, G, NZ * BLK, LANES), BF16), vm((2, NZ // 2, G, NY * BLK, LANES), BF16),
-            vm((2, G, NZ * BLK, LANES), BF16), vm((2, NZ // 2, G, NY * BLK, LANES), BF16),
+            vm((2, NY // 2, G, NZ * BLK, LANES), BF16), vm((2, NZ // 2, G, NY * BLK, LANES), BF16),
+            vm((2, NY // 2, G, NZ * BLK, LANES), BF16), vm((2, NZ // 2, G, NY * BLK, LANES), BF16),
             vm((NZ * PACK, LANES), F32), vm((NZ, PACK, LANES), BF16), vm((NZ, PACK, LANES), BF16),
             vm((PACK, LANES), F32), vm((PACK, LANES), F32), vm((NZ, PACK, LANES), BF16),
             vm((NZ * BLK, RANK), F32), vm((NZ * COLS, RANK), BF16),

time: 64.7 us -> 61.5 us (0.951); the launches traced: 63.9 us -> 61.4 us
  Pallas kernels: 63.2 us -> 60.8 us
    pallas_call x1, Pallas kernels: 62.5 us -> 60 us  [per_device(): pl.pallas_call(functools.partial(kernel, tokens=tokens), out_shape=(jax.S...]
where the time goes in v4:
time: 61.5 us; the launch traced here: 61.4 us
  Pallas kernels  60.8 us (99%)
  between operations  0.64 us (1%)
    pallas_call x1, Pallas kernels, per_device(): pl.pallas_call(functools.partial(kernel, tokens=tokens), out_shape=(jax.S...  60 us

profile of v4, /device:TPU:6, one launch (start us, length us, event | category | flops | bytes accessed | tf_op | source)
XLA Modules:
  0.0 61.4 jit_solution(16943056385919794047)
XLA Ops:
  0.6 60.0 %shard_map.94 = (bf16[64,1920]{1,0:T(8,128)(2,1)S(1)}, f32[20,512]{1,0:T(8,128)S(1)}, f32[20,512]{1,0:T(8,128)S(1)}) custom-call(bf16[320,1920]{1,0:T(8,128)(2,1)} %hid_hbm.1, bf16[320,6144]{1,0:T(8,128)(2,1)} %og_hbm.1, bf16[6144,512]{1,0:T(8,128)(2,1)} %bas_hbm.1, s32[20,512]{1,0:T(8,128)} %c1_hbm.1, f32[2,20]{1,0:T(2,128)} %bitcast.3, s32[20,512]{1,0:T(8,128)} %c2_hbm.1, ...), custom_call_target="tpu_custom_call" | custom-call | tf_op jit(solution)/shard_map/pallas_call | solution.py:344
  60.6 0.7 %shard_map.95 = (bf16[64,1920]{1,0:T(8,128)(2,1)}, f32[20,512]{1,0:T(8,128)}, f32[20,512]{1,0:T(8,128)}) custom-call(bf16[64,1920]{1,0:T(8,128)(2,1)S(1)} %get-tuple-element.9.wt, f32[20,512]{1,0:T(8,128)S(1)} %get-tuple-element.10.first_new, f32[20,512]{1,0:T(8,128)S(1)} %get-tuple-element.11.second_new), custom_call_target="tpu_custom_call" | custom-call | tf_op jit(solution)/shard_map/pallas_call | solution.py:372
